TPU v7x, 256 devices: a whole 4x4x8 slice. The times are simulated.
256 devices in a mesh: ctx: 32 (over z_hi, x, y), ch: 8 (over z_lo, core).
Axes of the slice: x: 4, y: 4, z: 8 (z_hi: 2, z_lo: 4; z = z_hi * 4 + z_lo), core: 2. Of those that a mesh axis runs over, the one named last changes fastest.
Arguments:
- query_proj: float32 [8192, 4096], P('ctx', 'ch'), may hold values from -6 to 6
- key_proj: float32 [8192, 4096], P('ctx', 'ch'), may hold values from -6 to 6
- value_proj: float32 [8192, 4096], P('ctx', 'ch'), may hold values from -6 to 6
- filter_taps: float32 [8192, 4096], P('ctx', 'ch'), may hold values from -0.0625 to 0.0625
- cotangent: float32 [8192, 4096], P('ctx', 'ch'), may hold values from -0.625 to 0.625
Outputs:
- output: float32 [8192, 4096], P('ctx', 'ch')
- grad_query: float32 [8192, 4096], P('ctx', 'ch')
- grad_key: float32 [8192, 4096], P('ctx', 'ch')
- grad_value: float32 [8192, 4096], P('ctx', 'ch')
- grad_filter: float32 [8192, 4096], P('ctx', 'ch')
All inputs are finite; a program needn't handle non-finite values.
Results may differ from a plain program's by a relative error of at most 0.0001.
Values sent between devices are 32-bit elements; how exact they have to be, the bound alone decides.
A program may use at most 128 MiB of HBM per device.

v0:
```python
import math

import jax
import jax.numpy as jnp
from jax import lax
from jax.sharding import PartitionSpec as P

HIGH = lax.Precision.HIGHEST


def counting(count):
    return jnp.arange(count, dtype=jnp.int32)


def angles(left_idx, right_idx, modulus):
    product = left_idx[:, None] * right_idx[None, :] % modulus
    turned = product.astype(jnp.float32) * jnp.float32(2.0 * math.pi / modulus)
    return (jnp.cos(turned), jnp.sin(turned))


def local_forward(signal):
    stacked, seq_len, narrow = signal.shape
    ctx_count = lax.axis_size("ctx")
    row_len = seq_len // ctx_count
    block_count = 2 * ctx_count
    padded_len = block_count * row_len
    grid = signal.reshape(stacked, ctx_count, row_len, narrow)
    cos_one, sin_one = angles(counting(block_count), counting(ctx_count), block_count)
    section_re = jnp.einsum("km,bmrc->bckr", cos_one, grid, precision=HIGH)
    section_im = -jnp.einsum("km,bmrc->bckr", sin_one, grid, precision=HIGH)
    cos_two, sin_two = angles(counting(block_count), counting(row_len), padded_len)
    cos_two = cos_two[None, None, :, :]
    sin_two = sin_two[None, None, :, :]
    turned_re = section_re * cos_two + section_im * sin_two
    turned_im = section_im * cos_two - section_re * sin_two
    cos_three, sin_three = angles(counting(row_len), counting(row_len), row_len)
    spec_re = jnp.einsum("qr,bckr->bckq", cos_three, turned_re, precision=HIGH) + jnp.einsum(
        "qr,bckr->bckq", sin_three, turned_im, precision=HIGH
    )
    spec_im = jnp.einsum("qr,bckr->bckq", cos_three, turned_im, precision=HIGH) - jnp.einsum(
        "qr,bckr->bckq", sin_three, turned_re, precision=HIGH
    )
    return (spec_re, spec_im)


def local_inverse(spec_re, spec_im):
    stacked, narrow, block_count, row_len = spec_re.shape
    ctx_count = block_count // 2
    padded_len = block_count * row_len
    cos_three, sin_three = angles(counting(row_len), counting(row_len), row_len)
    inner_re = jnp.einsum("rq,bckq->bckr", cos_three, spec_re, precision=HIGH) - jnp.einsum(
        "rq,bckq->bckr", sin_three, spec_im, precision=HIGH
    )
    inner_im = jnp.einsum("rq,bckq->bckr", cos_three, spec_im, precision=HIGH) + jnp.einsum(
        "rq,bckq->bckr", sin_three, spec_re, precision=HIGH
    )
    cos_two, sin_two = angles(counting(block_count), counting(row_len), padded_len)
    cos_two = cos_two[None, None, :, :]
    sin_two = sin_two[None, None, :, :]
    turned_re = inner_re * cos_two - inner_im * sin_two
    turned_im = inner_re * sin_two + inner_im * cos_two
    cos_one, sin_one = angles(counting(ctx_count), counting(block_count), block_count)
    rows_out = (
        jnp.einsum("mk,bckr->bmrc", cos_one, turned_re, precision=HIGH)
        - jnp.einsum("mk,bckr->bmrc", sin_one, turned_im, precision=HIGH)
    ) * jnp.float32(1.0 / padded_len)
    return rows_out.reshape(stacked, ctx_count * row_len, narrow)


def shards(query_proj, key_proj, value_proj, filter_taps, cotangent):
    mixed_in = key_proj * value_proj
    upstream = cotangent * query_proj
    outgoing = jnp.stack([mixed_in, filter_taps, upstream])
    arrived = lax.all_to_all(outgoing, "ctx", split_axis=2, concat_axis=1, tiled=True)
    spec_re, spec_im = local_forward(arrived)
    mix_re, mix_im = (spec_re[0], spec_im[0])
    tap_re, tap_im = (spec_re[1], spec_im[1])
    up_re, up_im = (spec_re[2], spec_im[2])
    back_re = jnp.stack(
        [
            mix_re * tap_re - mix_im * tap_im,
            tap_re * up_re + tap_im * up_im,
            mix_re * up_re + mix_im * up_im,
        ]
    )
    back_im = jnp.stack(
        [
            mix_re * tap_im + mix_im * tap_re,
            tap_re * up_im - tap_im * up_re,
            mix_re * up_im - mix_im * up_re,
        ]
    )
    results = local_inverse(back_re, back_im)
    returned = lax.all_to_all(results, "ctx", split_axis=1, concat_axis=2, tiled=True)
    convolved = returned[0]
    grad_mixed = returned[1]
    grad_taps = returned[2]
    output = query_proj * convolved
    grad_query = cotangent * convolved
    return (output, grad_query, grad_mixed * value_proj, grad_mixed * key_proj, grad_taps)


def solution(mesh):
    placed = (P("ctx", "ch"), P("ctx", "ch"), P("ctx", "ch"), P("ctx", "ch"), P("ctx", "ch"))
    return jax.shard_map(
        shards,
        mesh=mesh,
        in_specs=placed,
        out_specs=(P("ctx", "ch"), P("ctx", "ch"), P("ctx", "ch"), P("ctx", "ch"), P("ctx", "ch")),
        check_vma=False,
    )
```

profile of v0, /device:TPU:32, one launch (start us, length us, event | category | flops | bytes accessed | tf_op | source)
XLA Modules:
  0.0 218.1 jit_solution(1730528904660234190)
XLA Ops:
  0.7 1.3 copy.44
  2.0 1.4 copy.45
  3.4 0.1 mul.367
  3.5 0.4 stack.24
  3.9 0.3 copy-done.6
  4.2 0.2 copy.47
  4.5 0.2 copy.54
  4.7 0.1 mul.368
  4.7 0.4 stack.26
  5.1 0.4 copy.71
  5.5 2.7 %pad_maximum_fusion.6 = f32[3,256,512]{1,0,2:T(4,128)} fusion(f32[1,256,512]{1,0,2:T(1,128)S(1)} %stack.26, f32[1,256,512]{1,0,2:T(1,128)S(1)} %copy.71, f32[1,256,512]{1,0,2:T(1,128)S(1)} %stack.24), kind=kLoop, calls=%fused_computation.20 | loop fusion | flops 786432 | bytes 3145728 | tf_op jit(solution)/shard_map/stack | solution.py:73
  8.2 13.2 %all-to-all-start = ((f32[3,256,512]{1,0,2:T(4,128)}), f32[3,256,512]{1,0,2:T(4,128)S(1)}, u32[]{:S(2)}, u32[]{:S(2)}) async-start(f32[3,256,512]{1,0,2:T(4,128)} %pad_maximum_fusion.6), calls=%async_computation | async-start | bytes 4194304 | tf_op jit(solution)/shard_map/all_to_all | solution.py:74
  21.5 0.3 fusion.64
  21.7 52.7 %all-to-all-done = f32[3,256,512]{1,0,2:T(4,128)S(1)} async-done(((f32[3,256,512]{1,0,2:T(4,128)}), f32[3,256,512]{1,0,2:T(4,128)S(1)}, u32[]{:S(2)}, u32[]{:S(2)}) %all-to-all-start) | async-done | bytes 1572896 | tf_op jit(solution)/shard_map/all_to_all | solution.py:74
  74.4 3.7 %fusion.16 = f32[3,256,16,64]{1,3,2,0:T(8,128)S(1)} fusion(f32[3,256,32,16]{1,0,3,2:T(4,128)S(1)} %bitcast.91), kind=kOutput, calls=%fused_computation.25 | convolution fusion | flops 302018560 | bytes 4718592 | tf_op jit(solution)/shard_map/km,bmrc->bckr/dot_general | solution.py:30
  78.1 3.7 %fusion.18 = f32[3,256,16,64]{1,3,2,0:T(8,128)S(1)} fusion(f32[3,256,32,16]{1,0,3,2:T(4,128)S(1)} %bitcast.92), kind=kOutput, calls=%fused_computation.27 | convolution fusion | flops 302018560 | bytes 4718592 | tf_op jit(solution)/shard_map/km,bmrc->bckr/dot_general | solution.py:29
  81.8 3.8 %fusion.32 = f32[3,16,64,256]{3,2,1,0:T(8,128)S(1)} fusion(f32[3,256,16,64]{1,3,2,0:T(8,128)S(1)} %fusion.18, f32[3,256,16,64]{1,3,2,0:T(8,128)S(1)} %fusion.16, f32[64,256]{1,0:T(8,128)S(1)} %get-tuple-element.33, f32[64,256]{1,0:T(8,128)S(1)} %get-tuple-element.34), kind=kOutput, calls=%fused_computation.43 | convolution fusion | flops 2419982336 | bytes 9568256 | tf_op jit(solution)/shard_map/qr,bckr->bckq/dot_general | solution.py:37
  85.7 4.0 %fusion.28 = f32[3,16,64,256]{3,2,1,0:T(8,128)S(1)} fusion(f32[3,256,16,64]{1,3,2,0:T(8,128)S(1)} %fusion.18, f32[3,256,16,64]{1,3,2,0:T(8,128)S(1)} %fusion.16, f32[64,256]{1,0:T(8,128)S(1)} %get-tuple-element.33, f32[64,256]{1,0:T(8,128)S(1)} %get-tuple-element.34), kind=kOutput, calls=%fused_computation.42 | convolution fusion | flops 2419982336 | bytes 9568256 | tf_op jit(solution)/shard_map/qr,bckr->bckq/dot_general | solution.py:40
  89.6 3.9 %convolution_add_fusion = f32[3,16,64,256]{3,2,1,0:T(8,128)S(1)} fusion(f32[3,16,64,256]{3,2,1,0:T(8,128)S(1)} %fusion.32, f32[3,256,16,64]{1,3,2,0:T(8,128)S(1)} %fusion.18, f32[3,256,16,64]{1,3,2,0:T(8,128)S(1)} %fusion.16, f32[64,256]{1,0:T(8,128)S(1)} %get-tuple-element.33, f32[64,256]{1,0:T(8,128)S(1)} %get-tuple-element.34), kind=kOutput, calls=%fused_computation.22 | convolution fusion | flops 2420768768 | bytes 12713984 | tf_op jit(solution)/shard_map/qr,bckr->bckq/dot_general | solution.py:37
  93.6 3.9 %convolution_subtract_fusion = f32[3,16,64,256]{3,2,1,0:T(8,128)S(1)} fusion(f32[3,16,64,256]{3,2,1,0:T(8,128)S(1)} %fusion.28, f32[3,256,16,64]{1,3,2,0:T(8,128)S(1)} %fusion.18, f32[3,256,16,64]{1,3,2,0:T(8,128)S(1)} %fusion.16, f32[64,256]{1,0:T(8,128)S(1)} %get-tuple-element.33, f32[64,256]{1,0:T(8,128)S(1)} %get-tuple-element.34), kind=kOutput, calls=%fused_computation.21 | convolution fusion | flops 2420768768 | bytes 12713984 | tf_op jit(solution)/shard_map/qr,bckr->bckq/dot_general | solution.py:40
  97.4 0.7 multiply_add_fusion.2
  98.2 1.4 multiply_subtract_fusion.2
  99.6 3.7 %fusion.11 = f32[3,16,64,256]{3,2,1,0:T(8,128)S(1)} fusion(f32[1,16,64,256]{3,2,1,0:T(8,128)S(1)} %get-tuple-element.23, f32[1,16,64,256]{3,2,1,0:T(8,128)S(1)} %get-tuple-element.22, f32[1,16,64,256]{3,2,1,0:T(8,128)S(1)} %get-tuple-element.25), kind=kOutput, calls=%fused_computation.17 | convolution fusion | flops 2418409472 | bytes 6291456 | tf_op jit(solution)/shard_map/rq,bckq->bckr/dot_general | solution.py:51
  103.3 3.7 %fusion.10 = f32[3,16,64,256]{3,2,1,0:T(8,128)S(1)} fusion(f32[1,16,64,256]{3,2,1,0:T(8,128)S(1)} %get-tuple-element.23, f32[1,16,64,256]{3,2,1,0:T(8,128)S(1)} %get-tuple-element.22, f32[1,16,64,256]{3,2,1,0:T(8,128)S(1)} %get-tuple-element.25), kind=kOutput, calls=%fused_computation.16 | convolution fusion | flops 2418409472 | bytes 6291456 | tf_op jit(solution)/shard_map/rq,bckq->bckr/dot_general | solution.py:54
  107.0 3.9 %fusion.14 = f32[3,16,64,256]{3,2,1,0:T(8,128)S(1)} fusion(f32[3,16,64,256]{3,2,1,0:T(8,128)S(1)} %fusion.11, f32[1,16,64,256]{3,2,1,0:T(8,128)S(1)} %get-tuple-element.21, f32[1,16,64,256]{3,2,1,0:T(8,128)S(1)} %get-tuple-element.24, f32[1,16,64,256]{3,2,1,0:T(8,128)S(1)} %get-tuple-element.20), kind=kOutput, calls=%fused_computation.23 | convolution fusion | flops 2419195904 | bytes 9437184 | tf_op jit(solution)/shard_map/rq,bckq->bckr/dot_general | solution.py:51
  111.0 3.9 %fusion.15 = f32[3,16,64,256]{3,2,1,0:T(8,128)S(1)} fusion(f32[3,16,64,256]{3,2,1,0:T(8,128)S(1)} %fusion.10, f32[1,16,64,256]{3,2,1,0:T(8,128)S(1)} %get-tuple-element.21, f32[1,16,64,256]{3,2,1,0:T(8,128)S(1)} %get-tuple-element.24, f32[1,16,64,256]{3,2,1,0:T(8,128)S(1)} %get-tuple-element.20), kind=kOutput, calls=%fused_computation.24 | convolution fusion | flops 2419195904 | bytes 9437184 | tf_op jit(solution)/shard_map/rq,bckq->bckr/dot_general | solution.py:54
  114.9 2.4 %fusion.2 = f32[3,16,256,32]{2,3,1,0:T(8,128)S(1)} fusion(f32[3,16,64,256]{3,2,1,0:T(8,128)S(1)} %fusion.15, f32[3,16,64,256]{3,2,1,0:T(8,128)S(1)} %fusion.14, f32[64,256]{1,0:T(8,128)S(1)} %get-tuple-element.33, f32[64,256]{1,0:T(8,128)S(1)} %get-tuple-element.34), kind=kOutput, calls=%fused_computation.8 | convolution fusion | flops 304377856 | bytes 7995392 | tf_op jit(solution)/shard_map/mk,bckr->bmrc/dot_general | solution.py:65
  117.3 2.5 %multiply_bitcast_fusion = f32[3,32,256,16]{2,1,3,0:T(8,128)S(1)} fusion(f32[3,16,256,32]{2,3,1,0:T(8,128)S(1)} %fusion.2, f32[3,16,64,256]{3,2,1,0:T(8,128)S(1)} %fusion.15, f32[3,16,64,256]{3,2,1,0:T(8,128)S(1)} %fusion.14, f32[64,256]{1,0:T(8,128)S(1)} %get-tuple-element.33, f32[64,256]{1,0:T(8,128)S(1)} %get-tuple-element.34), kind=kOutput, calls=%fused_computation.29 | convolution fusion | flops 305164288 | bytes 9568256 | tf_op jit(solution)/shard_map/mk,bckr->bmrc/dot_general | solution.py:64
  119.8 8.6 %copy.74 = f32[3,32,256,16]{3,0,2,1:T(4,128)} copy(f32[3,32,256,16]{2,1,3,0:T(8,128)S(1)} %multiply_bitcast_fusion) | data formatting | bytes 3145728 | tf_op jit(solution)/shard_map/reshape | solution.py:67
  128.4 16.1 %reshape.64 = f32[32,1,12288]{2,1,0:T(1,128)S(1)} reshape(f32[8192,3,16]{2,1,0:T(4,128)} %bitcast.89) | data formatting | bytes 3145728
  144.5 39.2 %all_to_all.30 = f32[32,1,12288]{2,1,0:T(1,128)S(1)} all-to-all(f32[32,1,12288]{2,1,0:T(1,128)S(1)} %reshape.64), channel_id=1, replica_groups=mesh['ctx'=32,'ch'=8] {'ctx'}, dimensions={0} | all-to-all | bytes 3145728 | tf_op jit(solution)/shard_map/all_to_all | solution.py:94
  183.7 0.5 broadcast.172
  184.2 4.4 %reduce = f32[32,12288]{1,0:T(8,128)S(1)} reduce(f32[32,1,12288]{2,1,0:T(1,128)S(1)} %all_to_all.30, f32[]{:T(128)} %broadcast.172), dimensions={1}, to_apply=%all_to_all.25.reduce_sub_computation | reduce | bytes 3145732 | tf_op jit(solution)/shard_map/all_to_all | solution.py:94
  188.6 12.9 %reshape.65 = f32[8192,3,16]{2,1,0:T(4,128)} reshape(f32[32,12288]{1,0:T(8,128)S(1)} %reduce) | data formatting | bytes 3145728
  201.6 9.3 %copy.75 = f32[3,32,256,16]{2,1,3,0:T(8,128)S(1)} copy(f32[3,32,256,16]{3,0,2,1:T(4,128)} %bitcast.90) | data formatting | bytes 3145728 | tf_op jit(solution)/shard_map/all_to_all | solution.py:94
  210.9 0.2 fusion.142
  211.0 0.3 copy.56
  211.4 0.5 copy-done.5
  211.9 0.2 copy-done.7
  212.0 0.1 bitcast_multiply_fusion.4
  212.2 1.0 copy.62
  213.1 1.0 copy.63
  214.1 0.3 copy.53
  214.5 0.1 bitcast_multiply_fusion.6
  214.6 1.0 copy.60
  215.6 1.0 copy.61
  216.6 0.3 copy.59
  216.9 1.0 copy.64
  (19 shorter events, 0.1 us)
Async XLA Ops:
  0.6 3.6 %copy-start.8 = (f32[256,512]{1,0:T(8,128)S(1)}, f32[256,512]{1,0:T(8,128)}, u32[]{:S(2)}) copy-start(f32[256,512]{1,0:T(8,128)} %param.9) | copy-start | bytes 1572868
  0.6 3.8 %copy-start.9 = (f32[256,512]{1,0:T(8,128)S(1)}, f32[256,512]{1,0:T(8,128)}, u32[]{:S(2)}) copy-start(f32[256,512]{1,0:T(8,128)} %param.5) | copy-start | bytes 1572868
  2.0 1.5 copy-start.4
  3.4 0.8 copy-start.6
  3.5 1.6 copy-start.10
  4.4 3.8 %copy-start = (f32[256,512]{0,1:T(8,128)}, f32[256,512]{0,1:T(8,128)S(1)}, u32[]{:S(2)}) copy-start(f32[256,512]{0,1:T(8,128)S(1)} %copy.47) | copy-start | bytes 1572868
  4.7 3.6 %copy-start.2 = (f32[256,512]{0,1:T(8,128)}, f32[256,512]{0,1:T(8,128)S(1)}, u32[]{:S(2)}) copy-start(f32[256,512]{0,1:T(8,128)S(1)} %copy.54) | copy-start | bytes 1572868
  8.2 66.2 %all-to-all-start = ((f32[3,256,512]{1,0,2:T(4,128)}), f32[3,256,512]{1,0,2:T(4,128)S(1)}, u32[]{:S(2)}, u32[]{:S(2)}) async-start(f32[3,256,512]{1,0,2:T(4,128)} %pad_maximum_fusion.6), calls=%async_computation | async-start | bytes 4194304 | tf_op jit(solution)/shard_map/all_to_all | solution.py:74
  210.8 1.0 copy-start.5
  210.8 1.2 copy-start.7
  212.0 2.4 %copy-start.1 = (f32[256,512]{0,1:T(8,128)S(1)}, f32[256,512]{0,1:T(8,128)}, u32[]{:S(2)}) copy-start(f32[256,512]{0,1:T(8,128)} %copy-done) | copy-start | bytes 1572868
  212.0 2.4 %copy-start.3 = (f32[256,512]{0,1:T(8,128)S(1)}, f32[256,512]{0,1:T(8,128)}, u32[]{:S(2)}) copy-start(f32[256,512]{0,1:T(8,128)} %copy-done.2) | copy-start | bytes 1572868
where the time goes:
time: 222 us; the launch traced here: 218 us
  local copies, waits for them, and re-layouts  58.8 us (26%)
  waiting for transfers between devices  52.7 us (24%)
  matrix products  43.1 us (19%)
  blocking collectives  39.2 us (18%)
  starting transfers between devices  13.2 us (6%)
  other arithmetic  9.84 us (4%)
    all_to_all x1, waiting for transfers between devices, shards(): lax.all_to_all(outgoing, 'ctx', split_axis=2, concat_axis=1, tiled=True)  52.7 us
    all_to_all x1, blocking collectives, shards(): lax.all_to_all(results, 'ctx', split_axis=1, concat_axis=2, tiled=True)  39.2 us
    unnamed x33, local copies, waits for them, and re-layouts  38.2 us
    all_to_all x1, starting transfers between devices, shards(): lax.all_to_all(outgoing, 'ctx', split_axis=2, concat_axis=1, tiled=True)  13.2 us
    all_to_all x2, local copies, waits for them, and re-layouts, shards(): lax.all_to_all(results, 'ctx', split_axis=1, concat_axis=2, tiled=True)  9.78 us
    reshape x1, local copies, waits for them, and re-layouts, local_inverse(): return rows_out.reshape(stacked, ctx_count * row_len, narrow)  8.62 us
  transfers between devices with their start and end apart: 1, of which 1 were waited for; matrix products, arithmetic and copies ran while one was open for 0% of the time, Pallas kernels for 0%

commit v1 on v0

v1 whole, which is shorter than its diff:
```python
import functools
import math

import jax
import jax.numpy as jnp
import ml_dtypes
import numpy as np
from jax import lax
from jax.experimental import pallas as pl
from jax.experimental.pallas import tpu as pltpu
from jax.sharding import PartitionSpec as P

MESH = pl.DeviceIdType.MESH
BF16 = jnp.bfloat16
F32 = jnp.float32

BLOCKS = 32
ROW = 256
CHUNK = 8
CHUNKS = 2
SIDE = BLOCKS * CHUNK
PADDED = 2 * BLOCKS * ROW

PLANE = (
    (0, 1), (3, 0), (0, 3), (1, 0), (1, 1), (3, 3), (1, 3), (3, 1),
    (0, 2), (2, 0), (2, 1), (1, 2), (2, 3), (3, 2), (2, 2),
)
OFFSETS = ((1, 0, 0),) + tuple(o for dx, dy in PLANE for o in ((0, dx, dy), (1, dx, dy)))
PEERS = len(OFFSETS)


def split_np(values):
    high = values.astype(ml_dtypes.bfloat16)
    low = (values - high.astype(np.float64)).astype(ml_dtypes.bfloat16)
    return high, low


@functools.lru_cache(maxsize=None)
def tables():
    two_pi = 2.0 * math.pi
    half = np.arange(BLOCKS) + 0.5
    block = np.arange(BLOCKS)
    row = np.arange(ROW)
    eye = np.eye(CHUNK)
    psi = two_pi * np.outer(half, block) / (2 * BLOCKS)
    outer = np.concatenate([np.kron(np.cos(psi), eye), np.kron(-np.sin(psi), eye)], axis=0)
    high, low = split_np(outer)
    outer3 = np.concatenate([high, low, high], axis=1)
    theta = two_pi * np.outer(half, row) / PADDED
    turn_re = np.repeat(np.cos(theta), CHUNK, axis=0).astype(np.float32)
    turn_im = np.repeat(-np.sin(theta), CHUNK, axis=0).astype(np.float32)
    phi = two_pi * (np.outer(row, row) % ROW) / ROW
    inner = np.block([[np.cos(phi), -np.sin(phi)], [np.sin(phi), np.cos(phi)]])
    high, low = split_np(inner)
    inner3 = np.concatenate([high, high, low], axis=0)
    back = np.concatenate([np.kron(np.cos(psi.T), eye), np.kron(np.sin(psi.T), eye)], axis=1)
    high, low = split_np(back * (2.0 / PADDED))
    back3 = np.concatenate([high, low, high], axis=1)
    return outer3, turn_re, turn_im, inner3, back3


def halves(values):
    high = values.astype(BF16)
    return high, (values - high.astype(F32)).astype(BF16)


def transform(arrived, results, outer3, turn_re, turn_im, inner3, back3, wide):
    t_re = turn_re[...]
    t_im = turn_im[...]
    for sig in range(3):
        high, low = halves(arrived[:, sig].reshape(SIDE, ROW))
        mixed = jnp.dot(
            outer3[...], jnp.concatenate([high, high, low], axis=0), preferred_element_type=F32
        )
        z_re, z_im = mixed[:SIDE], mixed[SIDE:]
        rows = pl.ds(sig * SIDE, SIDE)
        high, low = halves(z_re * t_re - z_im * t_im)
        wide[rows, 0 * ROW : 1 * ROW] = high
        wide[rows, 2 * ROW : 3 * ROW] = low
        wide[rows, 4 * ROW : 5 * ROW] = high
        high, low = halves(z_re * t_im + z_im * t_re)
        wide[rows, 1 * ROW : 2 * ROW] = high
        wide[rows, 3 * ROW : 4 * ROW] = low
        wide[rows, 5 * ROW : 6 * ROW] = high
    spec = jnp.dot(wide[...], inner3[...], preferred_element_type=F32)
    m_re, m_im = spec[:SIDE, :ROW], spec[:SIDE, ROW:]
    h_re, h_im = spec[SIDE : 2 * SIDE, :ROW], spec[SIDE : 2 * SIDE, ROW:]
    u_re, u_im = spec[2 * SIDE :, :ROW], spec[2 * SIDE :, ROW:]
    products = (
        (m_re * h_re - m_im * h_im, -(m_re * h_im + m_im * h_re)),
        (h_re * u_re + h_im * u_im, h_im * u_re - h_re * u_im),
        (m_re * u_re + m_im * u_im, m_im * u_re - m_re * u_im),
    )
    for sig, (p_re, p_im) in enumerate(products):
        rows = pl.ds(sig * SIDE, SIDE)
        high, low = halves(p_re)
        wide[rows, 0 * ROW : 1 * ROW] = high
        wide[rows, 2 * ROW : 3 * ROW] = low
        wide[rows, 4 * ROW : 5 * ROW] = high
        high, low = halves(p_im)
        wide[rows, 1 * ROW : 2 * ROW] = high
        wide[rows, 3 * ROW : 4 * ROW] = low
        wide[rows, 5 * ROW : 6 * ROW] = high
    inv = jnp.dot(wide[...], inner3[...], preferred_element_type=F32)
    for sig in range(3):
        v_re = inv[sig * SIDE : (sig + 1) * SIDE, :ROW]
        v_im = inv[sig * SIDE : (sig + 1) * SIDE, ROW:]
        re_high, re_low = halves(v_re * t_re - v_im * t_im)
        im_high, im_low = halves(v_re * t_im + v_im * t_re)
        stacked = jnp.concatenate([re_high, im_high, re_high, im_high, re_low, im_low], axis=0)
        out = jnp.dot(back3[...], stacked, preferred_element_type=F32)
        results[:, sig] = out.reshape(BLOCKS, CHUNK, ROW)


def exchange_kernel(
    q_ref, k_ref, v_ref, f_ref, g_ref, outer_hbm, re_hbm, im_hbm, inner_hbm, back_hbm,
    returned,
    outgoing, arrived, results, wide, outer3, turn_re, turn_im, inner3, back3,
    table_sem, go_send, go_recv, back_send, back_recv, own_sem,
):
    ctx = lax.axis_index("ctx")
    ch = lax.axis_index("ch")
    z_hi = ctx // 16
    x = lax.rem(ctx // 4, 4)
    y = lax.rem(ctx, 4)
    peers = [
        lax.rem(z_hi + dz, 2) * 16 + lax.rem(x + dx, 4) * 4 + lax.rem(y + dy, 4)
        for dz, dx, dy in OFFSETS
    ]

    barrier = pltpu.get_barrier_semaphore()
    for peer in peers:
        pl.semaphore_signal(barrier, inc=1, device_id=(peer, ch), device_id_type=MESH)

    loads = [
        pltpu.make_async_copy(src, dst, table_sem.at[i])
        for i, (src, dst) in enumerate(
            (
                (outer_hbm, outer3), (re_hbm, turn_re), (im_hbm, turn_im),
                (inner_hbm, inner3), (back_hbm, back3),
            )
        )
    ]
    for load in loads:
        load.start()

    def prepare(chunk):
        lanes = pl.ds(chunk * SIDE, SIDE)
        signals = (
            k_ref[:, lanes] * v_ref[:, lanes],
            f_ref[:, lanes],
            g_ref[:, lanes] * q_ref[:, lanes],
        )
        for sig, values in enumerate(signals):
            outgoing[chunk, :, sig] = values.T.reshape(BLOCKS, CHUNK, ROW)
        arrived[chunk, ctx] = outgoing[chunk, ctx]

    def go(chunk, i):
        return pltpu.make_async_remote_copy(
            outgoing.at[chunk, peers[i]], arrived.at[chunk, ctx],
            go_send.at[chunk, i], go_recv.at[chunk, i],
            device_id=(peers[i], ch), device_id_type=MESH,
        )

    def come(chunk, i):
        return pltpu.make_async_remote_copy(
            results.at[chunk, peers[i]], returned.at[chunk, ctx],
            back_send.at[chunk, i], back_recv.at[chunk, i],
            device_id=(peers[i], ch), device_id_type=MESH,
        )

    def own(chunk):
        return pltpu.make_async_copy(
            results.at[chunk, ctx], returned.at[chunk, ctx], own_sem.at[chunk]
        )

    for chunk in range(CHUNKS):
        prepare(chunk)
        if chunk == 0:
            pl.semaphore_wait(barrier, PEERS)
        for i in range(PEERS):
            go(chunk, i).start()
    for load in loads:
        load.wait()
    for chunk in range(CHUNKS):
        for i in range(PEERS):
            go(chunk, i).wait_recv()
        transform(
            arrived.at[chunk], results.at[chunk], outer3, turn_re, turn_im, inner3, back3, wide
        )
        for i in range(PEERS):
            come(chunk, i).start()
        own(chunk).start()
    for chunk in range(CHUNKS):
        for i in range(PEERS):
            go(chunk, i).wait_send()
        own(chunk).wait()
        for i in range(PEERS):
            come(chunk, i).wait()


def exchange(query, key, value, taps, cotangent, *consts):
    vmem = pl.BlockSpec(memory_space=pltpu.VMEM)
    hbm = pl.BlockSpec(memory_space=pl.ANY)
    shape = (CHUNKS, BLOCKS, 3, CHUNK, ROW)
    return pl.pallas_call(
        exchange_kernel,
        out_shape=jax.ShapeDtypeStruct(shape, F32),
        in_specs=[vmem] * 5 + [hbm] * 5,
        out_specs=hbm,
        scratch_shapes=[
            pltpu.VMEM(shape, F32),
            pltpu.VMEM(shape, F32),
            pltpu.VMEM(shape, F32),
            pltpu.VMEM((3 * SIDE, 6 * ROW), BF16),
            *[pltpu.VMEM(c.shape, c.dtype) for c in consts],
            pltpu.SemaphoreType.DMA((5,)),
            pltpu.SemaphoreType.DMA((CHUNKS, PEERS)),
            pltpu.SemaphoreType.DMA((CHUNKS, PEERS)),
            pltpu.SemaphoreType.DMA((CHUNKS, PEERS)),
            pltpu.SemaphoreType.DMA((CHUNKS, PEERS)),
            pltpu.SemaphoreType.DMA((CHUNKS,)),
        ],
        compiler_params=pltpu.CompilerParams(
            collective_id=0, has_side_effects=True, vmem_limit_bytes=48 * 2**20
        ),
        name="exchange",
    )(query, key, value, taps, cotangent, *consts)


def gate_kernel(r_ref, q_ref, k_ref, v_ref, g_ref, out, d_query, d_key, d_value, d_taps):
    def turned(sig):
        return r_ref[0, :, sig].reshape(SIDE, -1).T

    convolved = turned(0)
    out[...] = q_ref[...] * convolved
    d_query[...] = g_ref[...] * convolved
    d_mixed = turned(1)
    d_key[...] = d_mixed * v_ref[...]
    d_value[...] = d_mixed * k_ref[...]
    d_taps[...] = turned(2)


def gate(returned, query, key, value, cotangent):
    part = 128
    block = pl.BlockSpec((part, SIDE), lambda c, p: (p, c))
    return pl.pallas_call(
        gate_kernel,
        grid=(CHUNKS, ROW // part),
        out_shape=[jax.ShapeDtypeStruct(query.shape, F32)] * 5,
        in_specs=[pl.BlockSpec((1, BLOCKS, 3, CHUNK, part), lambda c, p: (c, 0, 0, 0, p))]
        + [block] * 4,
        out_specs=[block] * 5,
        name="gate",
    )(returned, query, key, value, cotangent)


def shards(query, key, value, taps, cotangent):
    consts = [jnp.asarray(c) for c in tables()]
    returned = exchange(query, key, value, taps, cotangent, *consts)
    return tuple(gate(returned, query, key, value, cotangent))


def solution(mesh):
    placed = P("ctx", "ch")
    return jax.shard_map(
        shards,
        mesh=mesh,
        in_specs=(placed,) * 5,
        out_specs=(placed,) * 5,
        check_vma=False,
    )
```

time: 222 us -> 102 us (0.46)
  the two profiles are of different devices: /device:TPU:32 before, /device:TPU:64 now
where the time goes in v1:
time: 102 us; the launch traced here: 101 us
  Pallas kernels  91.3 us (90%)
  local copies, waits for them, and re-layouts  9.37 us (9%)
    pallas_call x1, Pallas kernels, exchange(): pl.pallas_call(exchange_kernel, out_shape=jax.ShapeDtypeStruct(shape, F32...  87 us
    unnamed x18, local copies, waits for them, and re-layouts  9.37 us
    pallas_call x1, Pallas kernels, gate(): pl.pallas_call(gate_kernel, grid=(CHUNKS, ROW // part), out_shape=[jax.Sh...  4.29 us

profile of v1, /device:TPU:64, one launch (start us, length us, event | category | flops | bytes accessed | tf_op | source)
XLA Modules:
  0.0 101.3 jit_solution(17031553412547820197)
XLA Ops:
  0.6 0.0 copy-start
  0.6 1.0 %copy-done = f32[256,512]{1,0:T(8,128)S(1)} copy-done((f32[256,512]{1,0:T(8,128)S(1)}, f32[256,512]{1,0:T(8,128)}, u32[]{:S(2)}) %copy-start) | copy-done | bytes 524312
  1.7 0.0 copy-start.1
  1.7 1.0 %copy-done.1 = f32[256,512]{1,0:T(8,128)S(1)} copy-done((f32[256,512]{1,0:T(8,128)S(1)}, f32[256,512]{1,0:T(8,128)}, u32[]{:S(2)}) %copy-start.1) | copy-done | bytes 524312
  2.7 0.0 copy-start.2
  2.7 1.0 %copy-done.2 = f32[256,512]{1,0:T(8,128)S(1)} copy-done((f32[256,512]{1,0:T(8,128)S(1)}, f32[256,512]{1,0:T(8,128)}, u32[]{:S(2)}) %copy-start.2) | copy-done | bytes 524312
  3.8 0.0 copy-start.3
  3.8 1.0 %copy-done.3 = f32[256,512]{1,0:T(8,128)S(1)} copy-done((f32[256,512]{1,0:T(8,128)S(1)}, f32[256,512]{1,0:T(8,128)}, u32[]{:S(2)}) %copy-start.3) | copy-done | bytes 524312
  4.8 0.0 copy-start.4
  4.8 1.1 %copy-done.4 = bf16[256,1536]{1,0:T(8,128)(2,1)S(1)} copy-done((bf16[256,1536]{1,0:T(8,128)(2,1)S(1)}, bf16[256,1536]{1,0:T(8,128)(2,1)}, u32[]{:S(2)}) %copy-start.4) | copy-done | bytes 786456
  5.9 0.0 copy-start.5
  5.9 1.1 %copy-done.5 = bf16[512,768]{1,0:T(8,128)(2,1)S(1)} copy-done((bf16[512,768]{1,0:T(8,128)(2,1)S(1)}, bf16[512,768]{1,0:T(8,128)(2,1)}, u32[]{:S(2)}) %copy-start.5) | copy-done | bytes 786456
  7.1 0.0 copy-start.6
  7.1 1.0 %copy-done.6 = f32[256,512]{1,0:T(8,128)S(1)} copy-done((f32[256,512]{1,0:T(8,128)S(1)}, f32[256,512]{1,0:T(8,128)}, u32[]{:S(2)}) %copy-start.6) | copy-done | bytes 524312
  8.1 0.0 copy-start.7
  8.1 0.9 copy-done.7
  9.1 0.0 copy-start.8
  9.1 0.9 copy-done.8
  10.0 87.0 %exchange.1.r_ref = f32[2,32,3,8,256]{4,3,2,1,0:T(8,128)} custom-call(f32[256,512]{1,0:T(8,128)S(1)} %copy-done, f32[256,512]{1,0:T(8,128)S(1)} %copy-done.1, f32[256,512]{1,0:T(8,128)S(1)} %copy-done.2, f32[256,512]{1,0:T(8,128)S(1)} %copy-done.6, f32[256,512]{1,0:T(8,128)S(1)} %copy-done.3, bf16[512,768]{1,0:T(8,128)(2,1)S(1)} %copy-done.5, ...), custom_call_target="tpu_custom_call" | custom-call | tf_op jit(solution)/shard_map/exchange/pallas_call | solution.py:206
  97.0 4.3 %gate.1 = (f32[256,512]{1,0:T(8,128)}, f32[256,512]{1,0:T(8,128)}, f32[256,512]{1,0:T(8,128)}, f32[256,512]{1,0:T(8,128)}, f32[256,512]{1,0:T(8,128)}) custom-call(f32[2,32,3,8,256]{4,3,2,1,0:T(8,128)} %exchange.1.r_ref, f32[256,512]{1,0:T(8,128)} %q_ref.3, f32[256,512]{1,0:T(8,128)} %k_ref.3, f32[256,512]{1,0:T(8,128)} %v_ref.3, f32[256,512]{1,0:T(8,128)} %g_ref.3), custom_call_target="tpu_custom_call" | custom-call | tf_op jit(solution)/shard_map/gate/pallas_call | solution.py:247
Async XLA Ops:
  0.6 1.0 %copy-start = (f32[256,512]{1,0:T(8,128)S(1)}, f32[256,512]{1,0:T(8,128)}, u32[]{:S(2)}) copy-start(f32[256,512]{1,0:T(8,128)} %q_ref.3) | copy-start | bytes 1572868
  1.7 1.0 %copy-start.1 = (f32[256,512]{1,0:T(8,128)S(1)}, f32[256,512]{1,0:T(8,128)}, u32[]{:S(2)}) copy-start(f32[256,512]{1,0:T(8,128)} %k_ref.3) | copy-start | bytes 1572868
  2.7 1.0 %copy-start.2 = (f32[256,512]{1,0:T(8,128)S(1)}, f32[256,512]{1,0:T(8,128)}, u32[]{:S(2)}) copy-start(f32[256,512]{1,0:T(8,128)} %v_ref.3) | copy-start | bytes 1572868
  3.8 1.0 %copy-start.3 = (f32[256,512]{1,0:T(8,128)S(1)}, f32[256,512]{1,0:T(8,128)}, u32[]{:S(2)}) copy-start(f32[256,512]{1,0:T(8,128)} %g_ref.3) | copy-start | bytes 1572868
  4.8 1.1 %copy-start.4 = (bf16[256,1536]{1,0:T(8,128)(2,1)S(1)}, bf16[256,1536]{1,0:T(8,128)(2,1)}, u32[]{:S(2)}) copy-start(bf16[256,1536]{1,0:T(8,128)(2,1)} %constant.14.clone.back_hbm) | copy-start | bytes 2359300
  5.9 1.1 %copy-start.5 = (bf16[512,768]{1,0:T(8,128)(2,1)S(1)}, bf16[512,768]{1,0:T(8,128)(2,1)}, u32[]{:S(2)}) copy-start(bf16[512,768]{1,0:T(8,128)(2,1)} %constant.10.clone.outer_hbm) | copy-start | bytes 2359300
  7.1 1.0 %copy-start.6 = (f32[256,512]{1,0:T(8,128)S(1)}, f32[256,512]{1,0:T(8,128)}, u32[]{:S(2)}) copy-start(f32[256,512]{1,0:T(8,128)} %f_ref.1) | copy-start | bytes 1572868
  8.1 0.9 copy-start.7
  9.1 0.9 copy-start.8

commit v2 on v1

--- a/solution.py
+++ b/solution.py
@@ -15,18 +15,21 @@
 F32 = jnp.float32
 
 BLOCKS = 32
+PLANES = 16
 ROW = 256
 CHUNK = 8
-CHUNKS = 2
+CHUNKS = 4
+LANES = PLANES * CHUNK
+FIRST = 0
+SECOND = tuple(c for c in range(CHUNKS) if c != FIRST)
 SIDE = BLOCKS * CHUNK
 PADDED = 2 * BLOCKS * ROW
 
-PLANE = (
+OFFSETS = (
     (0, 1), (3, 0), (0, 3), (1, 0), (1, 1), (3, 3), (1, 3), (3, 1),
-    (0, 2), (2, 0), (2, 1), (1, 2), (2, 3), (3, 2), (2, 2),
+    (0, 2), (2, 0), (2, 1), (1, 2), (2, 3), (3, 2), (2, 2), (0, 0),
 )
-OFFSETS = ((1, 0, 0),) + tuple(o for dx, dy in PLANE for o in ((0, dx, dy), (1, dx, dy)))
-PEERS = len(OFFSETS)
+NEAR = len(OFFSETS) - 1
 
 
 def split_np(values):
@@ -113,24 +116,47 @@
 
 
 def exchange_kernel(
-    q_ref, k_ref, v_ref, f_ref, g_ref, outer_hbm, re_hbm, im_hbm, inner_hbm, back_hbm,
-    returned,
-    outgoing, arrived, results, wide, outer3, turn_re, turn_im, inner3, back3,
-    table_sem, go_send, go_recv, back_send, back_recv, own_sem,
+    q_hbm, k_hbm, v_hbm, f_hbm, g_hbm, outer_hbm, re_hbm, im_hbm, inner_hbm, back_hbm,
+    returned, extra,
+    q_ref, k_ref, v_ref, f_ref, g_ref, outgoing, arrived, results,
+    wide, outer3, turn_re, turn_im, inner3, back3,
+    input_sem, table_sem, near_out, near_in, far_out, far_in,
+    near_back, near_home, far_back, far_home, own_sem,
 ):
     ctx = lax.axis_index("ctx")
     ch = lax.axis_index("ch")
-    z_hi = ctx // 16
-    x = lax.rem(ctx // 4, 4)
-    y = lax.rem(ctx, 4)
-    peers = [
-        lax.rem(z_hi + dz, 2) * 16 + lax.rem(x + dx, 4) * 4 + lax.rem(y + dy, 4)
-        for dz, dx, dy in OFFSETS
+    half = ctx // PLANES
+    place = lax.rem(ctx, PLANES)
+    x = place // 4
+    y = lax.rem(place, 4)
+    places = [lax.rem(x + dx, 4) * 4 + lax.rem(y + dy, 4) for dx, dy in OFFSETS]
+    here = half * PLANES
+    there = PLANES - here
+
+    pairs = (
+        (k_hbm, k_ref), (v_hbm, v_ref), (f_hbm, f_ref), (g_hbm, g_ref), (q_hbm, q_ref)
+    )
+    inputs = [
+        [
+            pltpu.make_async_copy(
+                src.at[:, pl.ds(chunk * LANES, LANES)], dst.at[chunk], input_sem.at[chunk, i]
+            )
+            for i, (src, dst) in enumerate(pairs)
+        ]
+        for chunk in range(CHUNKS)
     ]
+    for load in inputs[0] + inputs[1]:
+        load.start()
 
     barrier = pltpu.get_barrier_semaphore()
-    for peer in peers:
-        pl.semaphore_signal(barrier, inc=1, device_id=(peer, ch), device_id_type=MESH)
+    for i in range(NEAR + 1):
+        if i < NEAR:
+            pl.semaphore_signal(
+                barrier, inc=1, device_id=(here + places[i], ch), device_id_type=MESH
+            )
+        pl.semaphore_signal(
+            barrier, inc=1, device_id=(there + places[i], ch), device_id_type=MESH
+        )
 
     loads = [
         pltpu.make_async_copy(src, dst, table_sem.at[i])
@@ -141,124 +167,253 @@
             )
         )
     ]
-    for load in loads:
+    for load in inputs[2] + inputs[3] + loads:
         load.start()
 
-    def prepare(chunk):
-        lanes = pl.ds(chunk * SIDE, SIDE)
-        signals = (
-            k_ref[:, lanes] * v_ref[:, lanes],
-            f_ref[:, lanes],
-            g_ref[:, lanes] * q_ref[:, lanes],
-        )
-        for sig, values in enumerate(signals):
-            outgoing[chunk, :, sig] = values.T.reshape(BLOCKS, CHUNK, ROW)
-        arrived[chunk, ctx] = outgoing[chunk, ctx]
-
-    def go(chunk, i):
+    def near(chunk, i):
         return pltpu.make_async_remote_copy(
-            outgoing.at[chunk, peers[i]], arrived.at[chunk, ctx],
-            go_send.at[chunk, i], go_recv.at[chunk, i],
-            device_id=(peers[i], ch), device_id_type=MESH,
-        )
-
-    def come(chunk, i):
+            outgoing.at[chunk, places[i]], arrived.at[chunk, ctx],
+            near_out.at[chunk, i], near_in.at[chunk, i],
+            device_id=(here + places[i], ch), device_id_type=MESH,
+        )
+
+    def far(chunk, i):
+        count = 3 if chunk == FIRST else 2
         return pltpu.make_async_remote_copy(
-            results.at[chunk, peers[i]], returned.at[chunk, ctx],
-            back_send.at[chunk, i], back_recv.at[chunk, i],
-            device_id=(peers[i], ch), device_id_type=MESH,
+            outgoing.at[chunk, places[i], pl.ds(0, count)],
+            arrived.at[chunk, ctx, pl.ds(0, count)],
+            far_out.at[chunk, i], far_in.at[chunk, i],
+            device_id=(there + places[i], ch), device_id_type=MESH,
+        )
+
+    def near_return(chunk, i):
+        return pltpu.make_async_remote_copy(
+            results.at[chunk, here + places[i]], returned.at[chunk, place],
+            near_back.at[chunk, i], near_home.at[chunk, i],
+            device_id=(here + places[i], ch), device_id_type=MESH,
+        )
+
+    def far_return(chunk, i):
+        if chunk == FIRST:
+            src, dst = results.at[chunk, there + places[i]], returned.at[chunk, place]
+        else:
+            src = results.at[chunk, there + places[i], pl.ds(1, 2)]
+            dst = extra.at[chunk, place]
+        return pltpu.make_async_remote_copy(
+            src, dst, far_back.at[chunk, i], far_home.at[chunk, i],
+            device_id=(there + places[i], ch), device_id_type=MESH,
         )
 
     def own(chunk):
         return pltpu.make_async_copy(
-            results.at[chunk, ctx], returned.at[chunk, ctx], own_sem.at[chunk]
-        )
-
-    for chunk in range(CHUNKS):
-        prepare(chunk)
-        if chunk == 0:
-            pl.semaphore_wait(barrier, PEERS)
-        for i in range(PEERS):
-            go(chunk, i).start()
+            results.at[chunk, ctx], returned.at[chunk, place], own_sem.at[chunk]
+        )
+
+    def prepare(chunk):
+        for load in inputs[chunk]:
+            load.wait()
+        signals = (k_ref[chunk] * v_ref[chunk], f_ref[chunk], g_ref[chunk] * q_ref[chunk])
+        for sig, values in enumerate(signals):
+            outgoing[chunk, :, sig] = values.T.reshape(PLANES, CHUNK, ROW)
+        if chunk == FIRST:
+
+            @pl.when(half == 0)
+            def _():
+                arrived[chunk, ctx] = outgoing[chunk, place]
+        else:
+            arrived[chunk, ctx] = outgoing[chunk, place]
+
+    def start(copies):
+        for copy in copies:
+            copy.start()
+
+    def mingle(first, second):
+        order = []
+        for i in range(NEAR + 1):
+            order.append(first(i))
+            if i < NEAR:
+                order.append(second(i))
+        return order
+
+    def relay(done, follow):
+        for i in range(NEAR + 1):
+            done(i).wait_send()
+            follow(i).start()
+
+    def of(make, chunk):
+        return functools.partial(make, chunk)
+
+    def every(make, chunk):
+        return [make(chunk, i) for i in range(NEAR)]
+
+    def first_half(body):
+        pl.when(half == 0)(body)
+
+    def second_half(body):
+        pl.when(half == 1)(body)
+
+    @first_half
+    def _():
+        prepare(1)
+        pl.semaphore_wait(barrier, 2 * NEAR + 1)
+        prepare(0)
+        start(mingle(of(far, 1), of(near, 0)))
+        prepare(2)
+        prepare(3)
+        start(every(near, 1))
+        for chunk in SECOND:
+            arrived[chunk, PLANES:] = jnp.zeros((PLANES, 3, CHUNK, ROW), F32)
+
+    @second_half
+    def _():
+        prepare(0)
+        pl.semaphore_wait(barrier, 2 * NEAR + 1)
+        prepare(1)
+        start(mingle(of(far, 0), of(near, 1)))
+        prepare(2)
+        start(every(near, 2))
+        prepare(3)
+        start(every(near, 3))
+        for chunk in SECOND:
+            arrived[chunk, :PLANES, 2] = jnp.zeros((PLANES, CHUNK, ROW), F32)
+
     for load in loads:
         load.wait()
-    for chunk in range(CHUNKS):
-        for i in range(PEERS):
-            go(chunk, i).wait_recv()
+
+    def work(chunk):
+        for i in range(NEAR):
+            near(chunk, i).wait_recv()
         transform(
             arrived.at[chunk], results.at[chunk], outer3, turn_re, turn_im, inner3, back3, wide
         )
-        for i in range(PEERS):
-            come(chunk, i).start()
+        start(every(near_return, chunk))
         own(chunk).start()
-    for chunk in range(CHUNKS):
-        for i in range(PEERS):
-            go(chunk, i).wait_send()
+
+    def arrive(make, chunk):
+        for i in range(NEAR + 1):
+            make(chunk, i).wait_recv()
+
+    @first_half
+    def _():
+        relay(of(far, 1), of(far, 2))
+        start(every(near, 2))
+        arrive(far, 0)
+        work(0)
+        relay(of(far, 2), of(far, 3))
+        start(every(near, 3))
+
+    second_half(lambda: arrive(far, 1))
+    work(1)
+    second_half(lambda: relay(of(far, 0), of(far_return, 1)))
+
+    second_half(lambda: arrive(far, 2))
+    work(2)
+    first_half(lambda: relay(of(far, 3), of(far_return, 0)))
+    second_half(lambda: relay(of(far_return, 1), of(far_return, 2)))
+
+    second_half(lambda: arrive(far, 3))
+    work(3)
+    second_half(lambda: relay(of(far_return, 2), of(far_return, 3)))
+
+    def finish(chunk):
+        for i in range(NEAR):
+            near(chunk, i).wait_send()
+            near_return(chunk, i).wait()
         own(chunk).wait()
-        for i in range(PEERS):
-            come(chunk, i).wait()
+
+    for chunk in SECOND:
+        finish(chunk)
+
+    @first_half
+    def _():
+        finish(0)
+        for chunk in SECOND:
+            arrive(far_return, chunk)
+        for i in range(NEAR + 1):
+            far_return(0, i).wait_send()
+
+    @second_half
+    def _():
+        arrive(far_return, 0)
+        for i in range(NEAR + 1):
+            far_return(3, i).wait_send()
 
 
 def exchange(query, key, value, taps, cotangent, *consts):
-    vmem = pl.BlockSpec(memory_space=pltpu.VMEM)
     hbm = pl.BlockSpec(memory_space=pl.ANY)
-    shape = (CHUNKS, BLOCKS, 3, CHUNK, ROW)
+    signals = pltpu.VMEM((CHUNKS, BLOCKS, 3, CHUNK, ROW), F32)
+    near_sem = pltpu.SemaphoreType.DMA((CHUNKS, NEAR))
+    far_sem = pltpu.SemaphoreType.DMA((CHUNKS, NEAR + 1))
     return pl.pallas_call(
         exchange_kernel,
-        out_shape=jax.ShapeDtypeStruct(shape, F32),
-        in_specs=[vmem] * 5 + [hbm] * 5,
-        out_specs=hbm,
+        out_shape=[
+            jax.ShapeDtypeStruct((CHUNKS, PLANES, 3, CHUNK, ROW), F32),
+            jax.ShapeDtypeStruct((CHUNKS, PLANES, 2, CHUNK, ROW), F32),
+        ],
+        in_specs=[hbm] * 10,
+        out_specs=[hbm] * 2,
         scratch_shapes=[
-            pltpu.VMEM(shape, F32),
-            pltpu.VMEM(shape, F32),
-            pltpu.VMEM(shape, F32),
+            *[pltpu.VMEM((CHUNKS, ROW, LANES), F32)] * 5,
+            pltpu.VMEM((CHUNKS, PLANES, 3, CHUNK, ROW), F32),
+            signals,
+            signals,
             pltpu.VMEM((3 * SIDE, 6 * ROW), BF16),
             *[pltpu.VMEM(c.shape, c.dtype) for c in consts],
+            pltpu.SemaphoreType.DMA((CHUNKS, 5)),
             pltpu.SemaphoreType.DMA((5,)),
-            pltpu.SemaphoreType.DMA((CHUNKS, PEERS)),
-            pltpu.SemaphoreType.DMA((CHUNKS, PEERS)),
-            pltpu.SemaphoreType.DMA((CHUNKS, PEERS)),
-            pltpu.SemaphoreType.DMA((CHUNKS, PEERS)),
+            near_sem, near_sem, far_sem, far_sem, near_sem, near_sem, far_sem, far_sem,
             pltpu.SemaphoreType.DMA((CHUNKS,)),
         ],
         compiler_params=pltpu.CompilerParams(
-            collective_id=0, has_side_effects=True, vmem_limit_bytes=48 * 2**20
+            collective_id=0, has_side_effects=True, vmem_limit_bytes=60 * 2**20
         ),
         name="exchange",
     )(query, key, value, taps, cotangent, *consts)
 
 
-def gate_kernel(r_ref, q_ref, k_ref, v_ref, g_ref, out, d_query, d_key, d_value, d_taps):
-    def turned(sig):
-        return r_ref[0, :, sig].reshape(SIDE, -1).T
-
-    convolved = turned(0)
+def gate_kernel(r_ref, e_ref, q_ref, k_ref, v_ref, g_ref, out, d_query, d_key, d_value, d_taps):
+    chunk = pl.program_id(0)
+    shared = jnp.logical_and(lax.axis_index("ctx") < PLANES, chunk != FIRST)
+
+    def turned(ref, sig):
+        return ref[0, :, sig].reshape(LANES, -1).T
+
+    def summed(sig):
+        mine = turned(r_ref, sig)
+        return jnp.where(shared, mine + turned(e_ref, sig - 1), mine)
+
+    convolved = turned(r_ref, 0)
     out[...] = q_ref[...] * convolved
     d_query[...] = g_ref[...] * convolved
-    d_mixed = turned(1)
+    d_mixed = summed(1)
     d_key[...] = d_mixed * v_ref[...]
     d_value[...] = d_mixed * k_ref[...]
-    d_taps[...] = turned(2)
-
-
-def gate(returned, query, key, value, cotangent):
-    part = 128
-    block = pl.BlockSpec((part, SIDE), lambda c, p: (p, c))
+    d_taps[...] = summed(2)
+
+
+def gate(returned, extra, query, key, value, cotangent):
+    block = pl.BlockSpec((ROW, LANES), lambda c: (0, c))
     return pl.pallas_call(
         gate_kernel,
-        grid=(CHUNKS, ROW // part),
+        grid=(CHUNKS,),
         out_shape=[jax.ShapeDtypeStruct(query.shape, F32)] * 5,
-        in_specs=[pl.BlockSpec((1, BLOCKS, 3, CHUNK, part), lambda c, p: (c, 0, 0, 0, p))]
+        in_specs=[
+            pl.BlockSpec((1, PLANES, 3, CHUNK, ROW), lambda c: (c, 0, 0, 0, 0)),
+            pl.BlockSpec(
+                (1, PLANES, 2, CHUNK, ROW),
+                lambda c: (jnp.where(c == FIRST, FIRST + 1, c), 0, 0, 0, 0),
+            ),
+        ]
         + [block] * 4,
         out_specs=[block] * 5,
         name="gate",
-    )(returned, query, key, value, cotangent)
+    )(returned, extra, query, key, value, cotangent)
 
 
 def shards(query, key, value, taps, cotangent):
     consts = [jnp.asarray(c) for c in tables()]
-    returned = exchange(query, key, value, taps, cotangent, *consts)
-    return tuple(gate(returned, query, key, value, cotangent))
+    returned, extra = exchange(query, key, value, taps, cotangent, *consts)
+    return tuple(gate(returned, extra, query, key, value, cotangent))
 
 
 def solution(mesh):

time: 102 us -> 84.7 us (0.83)
  the two profiles are of different devices: /device:TPU:64 before, /device:TPU:32 now
where the time goes in v2:
time: 84.7 us; the launch traced here: 84.5 us
  Pallas kernels  83.8 us (99%)
    pallas_call x1, Pallas kernels, exchange(): pl.pallas_call(exchange_kernel, out_shape=[jax.ShapeDtypeStruct((CHUNKS,...  79.1 us
    pallas_call x1, Pallas kernels, gate(): pl.pallas_call(gate_kernel, grid=(CHUNKS,), out_shape=[jax.ShapeDtypeStru...  4.61 us

profile of v2, /device:TPU:32, one launch (start us, length us, event | category | flops | bytes accessed | tf_op | source)
XLA Modules:
  0.0 84.5 jit_solution(12854284300168250973)
XLA Ops:
  0.6 79.1 %exchange.1 = (f32[4,16,3,8,256]{4,3,2,1,0:T(8,128)}, f32[4,16,2,8,256]{4,3,2,1,0:T(8,128)}) custom-call(f32[256,512]{1,0:T(8,128)} %q_ref.1, f32[256,512]{1,0:T(8,128)} %k_ref.1, f32[256,512]{1,0:T(8,128)} %v_ref.1, f32[256,512]{1,0:T(8,128)} %f_hbm.1, f32[256,512]{1,0:T(8,128)} %g_ref.1, bf16[512,768]{1,0:T(8,128)(2,1)} %constant.10.clone.outer_hbm, ...), custom_call_target="tpu_custom_call" | custom-call | tf_op jit(solution)/shard_map/exchange/pallas_call | solution.py:347
  79.8 4.6 %gate.1 = (f32[256,512]{1,0:T(8,128)}, f32[256,512]{1,0:T(8,128)}, f32[256,512]{1,0:T(8,128)}, f32[256,512]{1,0:T(8,128)}, f32[256,512]{1,0:T(8,128)}) custom-call(f32[4,16,3,8,256]{4,3,2,1,0:T(8,128)} %get-tuple-element.7.r_ref, f32[4,16,2,8,256]{4,3,2,1,0:T(8,128)} %get-tuple-element.8.e_ref, f32[256,512]{1,0:T(8,128)} %q_ref.1, f32[256,512]{1,0:T(8,128)} %k_ref.1, ...), custom_call_target="tpu_custom_call" | custom-call | tf_op jit(solution)/shard_map/gate/pallas_call | solution.py:396

commit v3 on v2

--- a/solution.py
+++ b/solution.py
@@ -30,6 +30,8 @@
     (0, 2), (2, 0), (2, 1), (1, 2), (2, 3), (3, 2), (2, 2), (0, 0),
 )
 NEAR = len(OFFSETS) - 1
+COLUMN = 8
+PIECES = (tuple(range(8)), tuple(range(8, NEAR + 1)))
 
 
 def split_np(values):
@@ -121,7 +123,7 @@
     q_ref, k_ref, v_ref, f_ref, g_ref, outgoing, arrived, results,
     wide, outer3, turn_re, turn_im, inner3, back3,
     input_sem, table_sem, near_out, near_in, far_out, far_in,
-    near_back, near_home, far_back, far_home, own_sem,
+    near_back, near_home, far_back, far_home, own_sem, credit,
 ):
     ctx = lax.axis_index("ctx")
     ch = lax.axis_index("ch")
@@ -157,6 +159,11 @@
         pl.semaphore_signal(
             barrier, inc=1, device_id=(there + places[i], ch), device_id_type=MESH
         )
+    for k in range(1, COLUMN):
+        pl.semaphore_signal(
+            barrier, inc=1, device_id=(there + place, lax.rem(ch + k, COLUMN)),
+            device_id_type=MESH,
+        )
 
     loads = [
         pltpu.make_async_copy(src, dst, table_sem.at[i])
@@ -227,37 +234,39 @@
         for copy in copies:
             copy.start()
 
-    def mingle(first, second):
-        order = []
-        for i in range(NEAR + 1):
-            order.append(first(i))
-            if i < NEAR:
-                order.append(second(i))
-        return order
-
-    def relay(done, follow):
-        for i in range(NEAR + 1):
-            done(i).wait_send()
-            follow(i).start()
-
-    def of(make, chunk):
-        return functools.partial(make, chunk)
-
     def every(make, chunk):
         return [make(chunk, i) for i in range(NEAR)]
 
+    def part(make, chunk, piece):
+        return [make(chunk, i) for i in PIECES[piece]]
+
+    def grant(step):
+        for k in range(COLUMN):
+            pl.semaphore_signal(
+                credit.at[step], inc=1, device_id=(place, lax.rem(ch + k, COLUMN)),
+                device_id_type=MESH,
+            )
+
+    def granted(step, copies):
+        pl.semaphore_wait(credit.at[step], COLUMN)
+        start(copies)
+
     def first_half(body):
         pl.when(half == 0)(body)
 
     def second_half(body):
         pl.when(half == 1)(body)
+
+    def all_far(make, chunk):
+        return [make(chunk, i) for i in range(NEAR + 1)]
 
     @first_half
     def _():
         prepare(1)
-        pl.semaphore_wait(barrier, 2 * NEAR + 1)
+        pl.semaphore_wait(barrier, 2 * NEAR + COLUMN)
+        start(all_far(far, 1))
         prepare(0)
-        start(mingle(of(far, 1), of(near, 0)))
+        start(every(near, 0))
         prepare(2)
         prepare(3)
         start(every(near, 1))
@@ -267,9 +276,10 @@
     @second_half
     def _():
         prepare(0)
-        pl.semaphore_wait(barrier, 2 * NEAR + 1)
+        pl.semaphore_wait(barrier, 2 * NEAR + COLUMN)
+        start(all_far(far, 0))
         prepare(1)
-        start(mingle(of(far, 0), of(near, 1)))
+        start(every(near, 1))
         prepare(2)
         start(every(near, 2))
         prepare(3)
@@ -293,27 +303,39 @@
         for i in range(NEAR + 1):
             make(chunk, i).wait_recv()
 
+    def relay(done, follow):
+        for before, after in zip(done, follow):
+            before.wait_send()
+            after.start()
+
     @first_half
     def _():
-        relay(of(far, 1), of(far, 2))
+        relay(all_far(far, 1), all_far(far, 2))
         start(every(near, 2))
+        granted(0, all_far(far, 3))
+        start(every(near, 3))
         arrive(far, 0)
         work(0)
-        relay(of(far, 2), of(far, 3))
-        start(every(near, 3))
-
-    second_half(lambda: arrive(far, 1))
+
+    def come(chunk):
+        arrive(far, chunk)
+        if chunk == 1:
+            grant(0)
+        if chunk == 2:
+            grant(1)
+
+    second_half(lambda: come(1))
     work(1)
-    second_half(lambda: relay(of(far, 0), of(far_return, 1)))
-
-    second_half(lambda: arrive(far, 2))
+    second_half(lambda: start(all_far(far_return, 1)))
+    first_half(lambda: granted(1, all_far(far_return, 0)))
+
+    second_half(lambda: come(2))
     work(2)
-    first_half(lambda: relay(of(far, 3), of(far_return, 0)))
-    second_half(lambda: relay(of(far_return, 1), of(far_return, 2)))
-
-    second_half(lambda: arrive(far, 3))
+    second_half(lambda: start(all_far(far_return, 2)))
+
+    second_half(lambda: come(3))
     work(3)
-    second_half(lambda: relay(of(far_return, 2), of(far_return, 3)))
+    second_half(lambda: start(all_far(far_return, 3)))
 
     def finish(chunk):
         for i in range(NEAR):
@@ -329,14 +351,20 @@
         finish(0)
         for chunk in SECOND:
             arrive(far_return, chunk)
-        for i in range(NEAR + 1):
-            far_return(0, i).wait_send()
+            if chunk > 1:
+                for copy in all_far(far, chunk):
+                    copy.wait_send()
+        for copy in all_far(far_return, 0):
+            copy.wait_send()
 
     @second_half
     def _():
         arrive(far_return, 0)
-        for i in range(NEAR + 1):
-            far_return(3, i).wait_send()
+        for copy in all_far(far, 0):
+            copy.wait_send()
+        for chunk in SECOND:
+            for copy in all_far(far_return, chunk):
+                copy.wait_send()
 
 
 def exchange(query, key, value, taps, cotangent, *consts):
@@ -363,6 +391,7 @@
             pltpu.SemaphoreType.DMA((5,)),
             near_sem, near_sem, far_sem, far_sem, near_sem, near_sem, far_sem, far_sem,
             pltpu.SemaphoreType.DMA((CHUNKS,)),
+            pltpu.SemaphoreType.REGULAR((2,)),
         ],
         compiler_params=pltpu.CompilerParams(
             collective_id=0, has_side_effects=True, vmem_limit_bytes=60 * 2**20
@@ -371,41 +400,76 @@
     )(query, key, value, taps, cotangent, *consts)
 
 
-def gate_kernel(r_ref, e_ref, q_ref, k_ref, v_ref, g_ref, out, d_query, d_key, d_value, d_taps):
-    chunk = pl.program_id(0)
-    shared = jnp.logical_and(lax.axis_index("ctx") < PLANES, chunk != FIRST)
-
-    def turned(ref, sig):
-        return ref[0, :, sig].reshape(LANES, -1).T
-
-    def summed(sig):
-        mine = turned(r_ref, sig)
-        return jnp.where(shared, mine + turned(e_ref, sig - 1), mine)
-
-    convolved = turned(r_ref, 0)
-    out[...] = q_ref[...] * convolved
-    d_query[...] = g_ref[...] * convolved
-    d_mixed = summed(1)
-    d_key[...] = d_mixed * v_ref[...]
-    d_value[...] = d_mixed * k_ref[...]
-    d_taps[...] = summed(2)
+def gate_kernel(r_hbm, e_hbm, q_hbm, k_hbm, v_hbm, g_hbm, *rest):
+    outs_hbm = rest[:5]
+    r_ref, e_ref, q_ref, k_ref, v_ref, g_ref = rest[5:11]
+    outs = rest[11:16]
+    load_sem, store_sem = rest[16:]
+    shared = lax.axis_index("ctx") < PLANES
+
+    def lanes(ref, chunk):
+        return ref.at[:, pl.ds(chunk * LANES, LANES)]
+
+    def loads(chunk):
+        pairs = [(r_hbm.at[chunk], r_ref.at[chunk])]
+        if chunk != FIRST:
+            pairs.append((e_hbm.at[chunk], e_ref.at[chunk]))
+        for src, dst in ((q_hbm, q_ref), (g_hbm, g_ref), (v_hbm, v_ref), (k_hbm, k_ref)):
+            pairs.append((lanes(src, chunk), dst.at[chunk]))
+        return [
+            pltpu.make_async_copy(src, dst, load_sem.at[chunk, i])
+            for i, (src, dst) in enumerate(pairs)
+        ]
+
+    def stores(chunk):
+        return [
+            pltpu.make_async_copy(src.at[chunk], lanes(dst, chunk), store_sem.at[chunk, i])
+            for i, (src, dst) in enumerate(zip(outs, outs_hbm))
+        ]
+
+    for chunk in range(CHUNKS):
+        for load in loads(chunk):
+            load.start()
+    out, d_query, d_key, d_value, d_taps = outs
+    for chunk in range(CHUNKS):
+        for load in loads(chunk):
+            load.wait()
+
+        def summed(sig):
+            mine = r_ref[chunk, :, sig]
+            if chunk != FIRST:
+                mine = jnp.where(shared, mine + e_ref[chunk, :, sig - 1], mine)
+            return mine.reshape(LANES, ROW).T
+
+        convolved = r_ref[chunk, :, 0].reshape(LANES, ROW).T
+        out[chunk] = q_ref[chunk] * convolved
+        d_query[chunk] = g_ref[chunk] * convolved
+        d_mixed = summed(1)
+        d_key[chunk] = d_mixed * v_ref[chunk]
+        d_value[chunk] = d_mixed * k_ref[chunk]
+        d_taps[chunk] = summed(2)
+        for store in stores(chunk):
+            store.start()
+    for chunk in range(CHUNKS):
+        for store in stores(chunk):
+            store.wait()
 
 
 def gate(returned, extra, query, key, value, cotangent):
-    block = pl.BlockSpec((ROW, LANES), lambda c: (0, c))
+    hbm = pl.BlockSpec(memory_space=pl.ANY)
     return pl.pallas_call(
         gate_kernel,
-        grid=(CHUNKS,),
         out_shape=[jax.ShapeDtypeStruct(query.shape, F32)] * 5,
-        in_specs=[
-            pl.BlockSpec((1, PLANES, 3, CHUNK, ROW), lambda c: (c, 0, 0, 0, 0)),
-            pl.BlockSpec(
-                (1, PLANES, 2, CHUNK, ROW),
-                lambda c: (jnp.where(c == FIRST, FIRST + 1, c), 0, 0, 0, 0),
-            ),
-        ]
-        + [block] * 4,
-        out_specs=[block] * 5,
+        in_specs=[hbm] * 6,
+        out_specs=[hbm] * 5,
+        scratch_shapes=[
+            pltpu.VMEM(returned.shape, F32),
+            pltpu.VMEM(extra.shape, F32),
+            *[pltpu.VMEM((CHUNKS, ROW, LANES), F32)] * 9,
+            pltpu.SemaphoreType.DMA((CHUNKS, 6)),
+            pltpu.SemaphoreType.DMA((CHUNKS, 5)),
+        ],
+        compiler_params=pltpu.CompilerParams(vmem_limit_bytes=60 * 2**20),
         name="gate",
     )(returned, extra, query, key, value, cotangent)
 

time: 84.7 us -> 81.9 us (0.967)
  Pallas kernels: 83.8 us -> 81 us
    pallas_call x1, Pallas kernels: 79.1 us -> 77.2 us  [exchange(): pl.pallas_call(exchange_kernel, out_shape=[jax.ShapeDtypeStruct((CHUNKS,...]
where the time goes in v3:
time: 81.9 us; the launch traced here: 81.8 us
  Pallas kernels  81 us (99%)
    pallas_call x1, Pallas kernels, exchange(): pl.pallas_call(exchange_kernel, out_shape=[jax.ShapeDtypeStruct((CHUNKS,...  77.2 us
    pallas_call x1, Pallas kernels, gate(): pl.pallas_call(gate_kernel, out_shape=[jax.ShapeDtypeStruct(query.shape,...  3.81 us

profile of v3, /device:TPU:32, one launch (start us, length us, event | category | flops | bytes accessed | tf_op | source)
XLA Modules:
  0.0 81.8 jit_solution(8959830031712000382)
XLA Ops:
  0.6 77.2 %exchange.1 = (f32[4,16,3,8,256]{4,3,2,1,0:T(8,128)}, f32[4,16,2,8,256]{4,3,2,1,0:T(8,128)}) custom-call(f32[256,512]{1,0:T(8,128)} %q_hbm.3, f32[256,512]{1,0:T(8,128)} %k_hbm.3, f32[256,512]{1,0:T(8,128)} %v_hbm.3, f32[256,512]{1,0:T(8,128)} %f_hbm.1, f32[256,512]{1,0:T(8,128)} %g_hbm.3, bf16[512,768]{1,0:T(8,128)(2,1)} %constant.10.clone.outer_hbm, ...), custom_call_target="tpu_custom_call" | custom-call | tf_op jit(solution)/shard_map/exchange/pallas_call | solution.py:375
  77.9 3.8 %gate.1 = (f32[256,512]{1,0:T(8,128)}, f32[256,512]{1,0:T(8,128)}, f32[256,512]{1,0:T(8,128)}, f32[256,512]{1,0:T(8,128)}, f32[256,512]{1,0:T(8,128)}) custom-call(f32[4,16,3,8,256]{4,3,2,1,0:T(8,128)} %get-tuple-element.7.r_hbm, f32[4,16,2,8,256]{4,3,2,1,0:T(8,128)} %get-tuple-element.8.e_hbm, f32[256,512]{1,0:T(8,128)} %q_hbm.3, f32[256,512]{1,0:T(8,128)} %k_hbm.3, ...), custom_call_target="tpu_custom_call" | custom-call | tf_op jit(solution)/shard_map/gate/pallas_call | solution.py:460

commit v4 on v3

--- a/solution.py
+++ b/solution.py
@@ -26,8 +26,8 @@
 PADDED = 2 * BLOCKS * ROW
 
 OFFSETS = (
-    (0, 1), (3, 0), (0, 3), (1, 0), (1, 1), (3, 3), (1, 3), (3, 1),
-    (0, 2), (2, 0), (2, 1), (1, 2), (2, 3), (3, 2), (2, 2), (0, 0),
+    (2, 2), (1, 0), (0, 1), (2, 1), (3, 0), (0, 3), (2, 3), (1, 1),
+    (0, 2), (3, 3), (1, 2), (3, 1), (2, 0), (1, 3), (3, 2), (0, 0),
 )
 NEAR = len(OFFSETS) - 1
 COLUMN = 8
@@ -147,8 +147,18 @@
         ]
         for chunk in range(CHUNKS)
     ]
-    for load in inputs[0] + inputs[1]:
-        load.start()
+    def start(copies):
+        for copy in copies:
+            copy.start()
+
+    def first_half(body):
+        pl.when(half == 0)(body)
+
+    def second_half(body):
+        pl.when(half == 1)(body)
+
+    first_half(lambda: start(inputs[1]))
+    second_half(lambda: start(inputs[0]))
 
     barrier = pltpu.get_barrier_semaphore()
     for i in range(NEAR + 1):
@@ -174,8 +184,8 @@
             )
         )
     ]
-    for load in inputs[2] + inputs[3] + loads:
-        load.start()
+    first_half(lambda: start(inputs[0]))
+    second_half(lambda: start(inputs[1]))
 
     def near(chunk, i):
         return pltpu.make_async_remote_copy(
@@ -230,10 +240,6 @@
         else:
             arrived[chunk, ctx] = outgoing[chunk, place]
 
-    def start(copies):
-        for copy in copies:
-            copy.start()
-
     def every(make, chunk):
         return [make(chunk, i) for i in range(NEAR)]
 
@@ -251,12 +257,6 @@
         pl.semaphore_wait(credit.at[step], COLUMN)
         start(copies)
 
-    def first_half(body):
-        pl.when(half == 0)(body)
-
-    def second_half(body):
-        pl.when(half == 1)(body)
-
     def all_far(make, chunk):
         return [make(chunk, i) for i in range(NEAR + 1)]
 
@@ -265,6 +265,7 @@
         prepare(1)
         pl.semaphore_wait(barrier, 2 * NEAR + COLUMN)
         start(all_far(far, 1))
+        start(inputs[2] + inputs[3] + loads)
         prepare(0)
         start(every(near, 0))
         prepare(2)
@@ -278,6 +279,7 @@
         prepare(0)
         pl.semaphore_wait(barrier, 2 * NEAR + COLUMN)
         start(all_far(far, 0))
+        start(inputs[2] + inputs[3] + loads)
         prepare(1)
         start(every(near, 1))
         prepare(2)
@@ -349,13 +351,10 @@
     @first_half
     def _():
         finish(0)
+        for copy in all_far(far, 2) + all_far(far, 3) + all_far(far_return, 0):
+            copy.wait_send()
         for chunk in SECOND:
             arrive(far_return, chunk)
-            if chunk > 1:
-                for copy in all_far(far, chunk):
-                    copy.wait_send()
-        for copy in all_far(far_return, 0):
-            copy.wait_send()
 
     @second_half
     def _():

time: 81.9 us -> 80.9 us (0.988)
  the two profiles are of different devices: /device:TPU:32 before, /device:TPU:66 now
where the time goes in v4:
time: 80.9 us; the launch traced here: 80.8 us
  Pallas kernels  80 us (99%)
    pallas_call x1, Pallas kernels, exchange(): pl.pallas_call(exchange_kernel, out_shape=[jax.ShapeDtypeStruct((CHUNKS,...  76.2 us
    pallas_call x1, Pallas kernels, gate(): pl.pallas_call(gate_kernel, out_shape=[jax.ShapeDtypeStruct(query.shape,...  3.81 us

profile of v4, /device:TPU:66, one launch (start us, length us, event | category | flops | bytes accessed | tf_op | source)
XLA Modules:
  0.0 80.8 jit_solution(18122982693564449391)
XLA Ops:
  0.6 76.2 %exchange.1 = (f32[4,16,3,8,256]{4,3,2,1,0:T(8,128)}, f32[4,16,2,8,256]{4,3,2,1,0:T(8,128)}) custom-call(f32[256,512]{1,0:T(8,128)} %q_hbm.3, f32[256,512]{1,0:T(8,128)} %k_hbm.3, f32[256,512]{1,0:T(8,128)} %v_hbm.3, f32[256,512]{1,0:T(8,128)} %f_hbm.1, f32[256,512]{1,0:T(8,128)} %g_hbm.3, bf16[512,768]{1,0:T(8,128)(2,1)} %constant.10.clone.outer_hbm, ...), custom_call_target="tpu_custom_call" | custom-call | tf_op jit(solution)/shard_map/exchange/pallas_call | solution.py:374
  76.8 3.8 %gate.1 = (f32[256,512]{1,0:T(8,128)}, f32[256,512]{1,0:T(8,128)}, f32[256,512]{1,0:T(8,128)}, f32[256,512]{1,0:T(8,128)}, f32[256,512]{1,0:T(8,128)}) custom-call(f32[4,16,3,8,256]{4,3,2,1,0:T(8,128)} %get-tuple-element.7.r_hbm, f32[4,16,2,8,256]{4,3,2,1,0:T(8,128)} %get-tuple-element.8.e_hbm, f32[256,512]{1,0:T(8,128)} %q_hbm.3, f32[256,512]{1,0:T(8,128)} %k_hbm.3, ...), custom_call_target="tpu_custom_call" | custom-call | tf_op jit(solution)/shard_map/gate/pallas_call | solution.py:459

commit v5 on v4

--- a/solution.py
+++ b/solution.py
@@ -26,8 +26,7 @@
 PADDED = 2 * BLOCKS * ROW
 
 OFFSETS = (
-    (2, 2), (1, 0), (0, 1), (2, 1), (3, 0), (0, 3), (2, 3), (1, 1),
-    (0, 2), (3, 3), (1, 2), (3, 1), (2, 0), (1, 3), (3, 2), (0, 0),
+    (2, 2), (1, 2), (2, 1), (2, 3), (3, 2), (0, 2), (1, 1), (1, 3), (2, 0), (3, 1), (3, 3), (0, 1), (0, 3), (1, 0), (3, 0), (0, 0),
 )
 NEAR = len(OFFSETS) - 1
 COLUMN = 8

time: 80.9 us -> 79.7 us (0.985)
  the two profiles are of different devices: /device:TPU:66 before, /device:TPU:32 now
where the time goes in v5:
time: 79.7 us; the launch traced here: 78.5 us
  Pallas kernels  77.7 us (97%)
  between operations  0.8 us (1%)
    pallas_call x1, Pallas kernels, exchange(): pl.pallas_call(exchange_kernel, out_shape=[jax.ShapeDtypeStruct((CHUNKS,...  73.9 us
    pallas_call x1, Pallas kernels, gate(): pl.pallas_call(gate_kernel, out_shape=[jax.ShapeDtypeStruct(query.shape,...  3.81 us

profile of v5, /device:TPU:32, one launch (start us, length us, event | category | flops | bytes accessed | tf_op | source)
XLA Modules:
  0.0 78.5 jit_solution(6397491557900741279)
XLA Ops:
  0.6 73.9 %exchange.1 = (f32[4,16,3,8,256]{4,3,2,1,0:T(8,128)}, f32[4,16,2,8,256]{4,3,2,1,0:T(8,128)}) custom-call(f32[256,512]{1,0:T(8,128)} %q_hbm.3, f32[256,512]{1,0:T(8,128)} %k_hbm.3, f32[256,512]{1,0:T(8,128)} %v_hbm.3, f32[256,512]{1,0:T(8,128)} %f_hbm.1, f32[256,512]{1,0:T(8,128)} %g_hbm.3, bf16[512,768]{1,0:T(8,128)(2,1)} %constant.10.clone.outer_hbm, ...), custom_call_target="tpu_custom_call" | custom-call | tf_op jit(solution)/shard_map/exchange/pallas_call | solution.py:373
  74.5 3.8 %gate.1 = (f32[256,512]{1,0:T(8,128)}, f32[256,512]{1,0:T(8,128)}, f32[256,512]{1,0:T(8,128)}, f32[256,512]{1,0:T(8,128)}, f32[256,512]{1,0:T(8,128)}) custom-call(f32[4,16,3,8,256]{4,3,2,1,0:T(8,128)} %get-tuple-element.7.r_hbm, f32[4,16,2,8,256]{4,3,2,1,0:T(8,128)} %get-tuple-element.8.e_hbm, f32[256,512]{1,0:T(8,128)} %q_hbm.3, f32[256,512]{1,0:T(8,128)} %k_hbm.3, ...), custom_call_target="tpu_custom_call" | custom-call | tf_op jit(solution)/shard_map/gate/pallas_call | solution.py:458
